TPU v7x, 256 devices: a whole 4x4x8 slice. The times are simulated.
256 devices in a mesh: rep: 2 (over y_lo), seq: 64 (over x, z, core), chan: 2 (over y_hi).
Axes of the slice: x: 4, y: 4 (y_hi: 2, y_lo: 2; y = y_hi * 2 + y_lo), z: 8, core: 2. Of those that a mesh axis runs over, the one named last changes fastest.
Arguments:
- inputs: bfloat16 [2, 65536, 256], P('rep', 'seq', 'chan'), may hold values from -6 to 6
- cotangent: bfloat16 [2, 65536, 256], P('rep', 'seq', 'chan'), may hold values from -0.015625 to 0.015625
- filter_taps: bfloat16 [65536, 256], P('seq', 'chan'), may hold values from -6 to 6
- out_proj: bfloat16 [256, 256], P('chan'), may hold values from -0.375 to 0.375
Outputs:
- grad_input: bfloat16 [2, 65536, 256], P('rep', 'seq', 'chan')
- grad_filter: float32 [65536, 256], P('seq', 'chan')
All inputs are finite; a program needn't handle non-finite values.
Results may differ from a plain program's by a relative error of at most 0.0049.
Values may be sent and summed in bfloat16 or wider, within the bound.
A program may use at most 128 MiB of HBM per device.

v0:
```python
import math
import jax
import jax.numpy as jnp
from jax import lax
from jax.sharding import PartitionSpec as P

FACTOR = 16
precise_mode = lax.Precision.HIGHEST


def angle_table(numerator, modulus):
    return (numerator % modulus).astype(jnp.float32) * (2.0 * math.pi / modulus)


def dft_table(table_size, direction):
    index_row = jnp.arange(table_size, dtype=jnp.int32)
    angle_grid = angle_table(index_row[:, None] * index_row[None, :], table_size)
    return (jnp.cos(angle_grid), direction * jnp.sin(angle_grid))


def complex_apply(pattern, matrix, real_part, imag_part):
    matrix_real, matrix_imag = matrix

    def product(first_op, second_op):
        return jnp.einsum(pattern, first_op, second_op, precision=precise_mode)

    return (
        product(matrix_real, real_part) - product(matrix_imag, imag_part),
        product(matrix_real, imag_part) + product(matrix_imag, real_part),
    )


def rotate(real_part, imag_part, angle_grid, direction):
    cosine = jnp.cos(angle_grid)
    sine_part = direction * jnp.sin(angle_grid)
    return (real_part * cosine - imag_part * sine_part, real_part * sine_part + imag_part * cosine)


def twist_signal(values, positions, seq_length):
    angle_grid = angle_table(positions, 2 * seq_length)[:, :, None]
    real_part = jnp.stack([values, values * jnp.cos(angle_grid)])
    imag_part = jnp.stack([jnp.zeros_like(values), -values * jnp.sin(angle_grid)])
    return (real_part, imag_part)


def untwist(real_part, imag_part, positions, seq_length):
    angle_grid = angle_table(positions, 2 * seq_length)[:, :, None]
    running = real_part[0] + real_part[1] * jnp.cos(angle_grid) - imag_part[1] * jnp.sin(angle_grid)
    return running / (2.0 * seq_length)


def twiddle_rows(real_part, imag_part, freq_index, row_index, seq_length, direction):
    angle_grid = angle_table(freq_index[:, None] * row_index[None, :], seq_length)[None, :, :, None]
    return rotate(real_part, imag_part, angle_grid, direction)


def rows_forward(real_part, imag_part):
    twists, groups, tok_rows, part_width = real_part.shape
    outer_size = tok_rows // FACTOR
    real_part = real_part.reshape(twists, groups, outer_size, FACTOR, part_width)
    imag_part = imag_part.reshape(twists, groups, outer_size, FACTOR, part_width)
    real_part, imag_part = complex_apply(
        "qr,bkrsc->bkqsc", dft_table(outer_size, -1.0), real_part, imag_part
    )
    outer_index = jnp.arange(outer_size, dtype=jnp.int32)
    inner_index = jnp.arange(FACTOR, dtype=jnp.int32)
    angle_grid = angle_table(outer_index[:, None] * inner_index[None, :], tok_rows)[
        None, None, :, :, None
    ]
    real_part, imag_part = rotate(real_part, imag_part, angle_grid, -1.0)
    return complex_apply("ps,bkqsc->bkqpc", dft_table(FACTOR, -1.0), real_part, imag_part)


def rows_inverse(real_part, imag_part):
    twists, groups, outer_size, inner_size, part_width = real_part.shape
    tok_rows = outer_size * inner_size
    real_part, imag_part = complex_apply(
        "sp,bkqpc->bkqsc", dft_table(inner_size, 1.0), real_part, imag_part
    )
    outer_index = jnp.arange(outer_size, dtype=jnp.int32)
    inner_index = jnp.arange(inner_size, dtype=jnp.int32)
    angle_grid = angle_table(outer_index[:, None] * inner_index[None, :], tok_rows)[
        None, None, :, :, None
    ]
    real_part, imag_part = rotate(real_part, imag_part, angle_grid, 1.0)
    real_part, imag_part = complex_apply(
        "rq,bkqsc->bkrsc", dft_table(outer_size, 1.0), real_part, imag_part
    )
    return (
        real_part.reshape(twists, groups, tok_rows, part_width),
        imag_part.reshape(twists, groups, tok_rows, part_width),
    )


def conj_product(first_real, first_imag, second_real, second_imag):
    return (
        first_real * second_real + first_imag * second_imag,
        first_imag * second_real - first_real * second_imag,
    )


def per_device(inputs, cotangent, filter_taps, out_proj):
    devices = lax.axis_size("seq")
    seq_index = lax.axis_index("seq")
    tok_rows = inputs.shape[1]
    chan_width = inputs.shape[2]
    seq_length = devices * tok_rows
    grad_seq = cotangent.reshape(tok_rows, chan_width)
    projected = lax.dot_general(
        lax.all_gather(grad_seq, "chan", axis=1, tiled=True),
        out_proj,
        (((1,), (1,)), ((), ())),
        preferred_element_type=jnp.float32,
    )
    grad_mixed = projected.astype(jnp.bfloat16)
    signals = (grad_mixed, inputs.reshape(tok_rows, chan_width), filter_taps)
    device_index = jnp.arange(devices, dtype=jnp.int32)
    block_rows = tok_rows // devices
    pieces = (
        lax.all_to_all(signals[0], "seq", split_axis=0, concat_axis=0, tiled=True),
        lax.all_to_all(signals[1], "seq", split_axis=0, concat_axis=0, tiled=True),
        lax.all_to_all(signals[2], "seq", split_axis=0, concat_axis=0, tiled=True),
    )
    stacked = jnp.concatenate([member.astype(jnp.float32) for member in pieces], axis=1)
    stacked = stacked.reshape(devices, block_rows, 3 * chan_width)
    local_rows = seq_index * block_rows + jnp.arange(block_rows, dtype=jnp.int32)
    positions = device_index[:, None] * tok_rows + local_rows[None, :]
    real_part, imag_part = twist_signal(stacked, positions, seq_length)
    real_part, imag_part = complex_apply(
        "kp,bpsc->bksc", dft_table(devices, -1.0), real_part, imag_part
    )
    real_part, imag_part = twiddle_rows(
        real_part, imag_part, device_index, local_rows, seq_length, -1.0
    )
    real_part, imag_part = (
        lax.all_to_all(real_part, "seq", split_axis=1, concat_axis=2, tiled=True),
        lax.all_to_all(imag_part, "seq", split_axis=1, concat_axis=2, tiled=True),
    )
    real_part, imag_part = rows_forward(real_part, imag_part)
    part_width = real_part.shape[-1] // 3
    grad_real = real_part[..., :part_width]
    grad_imag = imag_part[..., :part_width]
    input_real = real_part[..., part_width : 2 * part_width]
    input_imag = imag_part[..., part_width : 2 * part_width]
    taps_real = real_part[..., 2 * part_width :]
    taps_imag = imag_part[..., 2 * part_width :]
    du_real, du_imag = conj_product(grad_real, grad_imag, taps_real, taps_imag)
    dk_real, dk_imag = conj_product(grad_real, grad_imag, input_real, input_imag)
    dk_real, dk_imag = lax.psum((dk_real, dk_imag), "rep")
    joined_real = jnp.concatenate([du_real, dk_real], axis=4)
    joined_imag = jnp.concatenate([du_imag, dk_imag], axis=4)
    real_part, imag_part = rows_inverse(joined_real, joined_imag)
    freq_here = jnp.reshape(seq_index, (1,))
    all_rows = jnp.arange(tok_rows, dtype=jnp.int32)
    real_part, imag_part = twiddle_rows(real_part, imag_part, freq_here, all_rows, seq_length, 1.0)
    real_part, imag_part = (
        lax.all_to_all(real_part, "seq", split_axis=2, concat_axis=1, tiled=True),
        lax.all_to_all(imag_part, "seq", split_axis=2, concat_axis=1, tiled=True),
    )
    real_part, imag_part = complex_apply(
        "pk,bksc->bpsc", dft_table(devices, 1.0), real_part, imag_part
    )
    values = untwist(real_part, imag_part, positions, seq_length)
    grad_rows = values[:, :, :part_width].astype(jnp.bfloat16).reshape(tok_rows, part_width)
    grad_input = lax.all_to_all(grad_rows, "seq", split_axis=0, concat_axis=0, tiled=True)
    filter_rows = values[:, :, part_width:].reshape(tok_rows, values.shape[2] - part_width)
    grad_filter = lax.all_to_all(filter_rows, "seq", split_axis=0, concat_axis=0, tiled=True)
    return (grad_input.reshape(1, tok_rows, chan_width), grad_filter)


def solution(mesh):
    return jax.shard_map(
        per_device,
        mesh=mesh,
        in_specs=(
            P("rep", "seq", "chan"),
            P("rep", "seq", "chan"),
            P("seq", "chan"),
            P("chan", None),
        ),
        out_specs=(P("rep", "seq", "chan"), P("seq", "chan")),
        check_vma=False,
    )
```

profile of v0, /device:TPU:1, one launch (start us, length us, event | category | flops | bytes accessed | tf_op | source)
XLA Modules:
  0.0 586.2 jit_solution(16802311897165362928)
XLA Ops:
  7.2 9.9 %all-gather = bf16[1,1024,256]{2,1,0:T(8,128)(2,1)S(1)} all-gather(bf16[1,1024,128]{2,1,0:T(8,128)(2,1)} %param.5), channel_id=2, replica_groups=mesh['rep'=2,'seq'=64,'chan'=2] {'chan'}, dimensions={2}, use_global_device_ids=true | all-gather | bytes 786432 | tf_op jit(solution)/shard_map/all_gather | solution.py:110
  17.4 25.4 %all_to_all.84 = bf16[64,16,128]{2,1,0:T(8,128)(2,1)S(1)} all-to-all(bf16[64,16,128]{2,1,0:T(8,128)(2,1)S(1)} %bitcast.244), channel_id=1, replica_groups=mesh['rep'=2,'seq'=64,'chan'=2] {'seq'}, dimensions={0} | all-to-all | bytes 524288 | tf_op jit(solution)/shard_map/all_to_all | solution.py:120
  42.9 17.8 %all_to_all.85 = bf16[64,16,128]{2,1,0:T(8,128)(2,1)S(1)} all-to-all(bf16[64,16,128]{2,1,0:T(8,128)(2,1)S(1)} %bitcast.245), channel_id=1, replica_groups=mesh['rep'=2,'seq'=64,'chan'=2] {'seq'}, dimensions={0} | all-to-all | bytes 524288 | tf_op jit(solution)/shard_map/all_to_all | solution.py:122
  60.7 6.5 %all-to-all-start.1 = ((bf16[64,16,128]{2,1,0:T(8,128)(2,1)}), bf16[64,16,128]{2,1,0:T(8,128)(2,1)S(1)}, u32[]{:S(2)}, u32[]{:S(2)}) async-start(bf16[64,16,128]{2,1,0:T(8,128)(2,1)} %bitcast.3), calls=%async_computation.1 | async-start | bytes 524288 | tf_op jit(solution)/shard_map/all_to_all | solution.py:121
  67.5 11.5 %all-to-all-done.1 = bf16[64,16,128]{2,1,0:T(8,128)(2,1)S(1)} async-done(((bf16[64,16,128]{2,1,0:T(8,128)(2,1)}), bf16[64,16,128]{2,1,0:T(8,128)(2,1)S(1)}, u32[]{:S(2)}, u32[]{:S(2)}) %all-to-all-start.1) | async-done | bytes 262176 | tf_op jit(solution)/shard_map/all_to_all | solution.py:121
  87.5 17.7 %fusion.4 = (f32[2,64,16,384]{3,1,2,0:T(8,128)}, f32[2,64,16,384]{3,1,2,0:T(8,128)S(1)}) fusion(f32[2,16,384,64]{2,3,1,0:T(8,128)S(1)} %fusion.56, f32[64,16]{0,1:T(8,128)S(1)} %get-tuple-element.19, f32[64,16]{0,1:T(8,128)S(1)} %get-tuple-element.18, f32[2,16,384,64]{2,3,1,0:T(8,128)S(1)} %fusion.73, f32[1,64,16,384]{3,1,2,0:T(8,128)S(1)} %convert_multiply_fusion, ...), kind=kOutput, calls=%fused_computation.11 | convolution fusion | flops 610332672 | bytes 15736832 | tf_op jit(solution)/shard_map/kp,bpsc->bksc/dot_general | solution.py:25
  105.3 3.5 copy.43
  108.8 6.0 %all-to-all-start.4 = ((f32[2,64,16,384]{3,2,0,1:T(8,128)}), f32[2,64,16,384]{3,2,0,1:T(8,128)S(1)}, u32[]{:S(2)}, u32[]{:S(2)}) async-start(f32[2,64,16,384]{3,2,0,1:T(8,128)} %copy.43), calls=%async_computation.4 | async-start | bytes 6291456 | tf_op jit(solution)/shard_map/all_to_all | solution.py:137
  114.8 5.3 copy.41
  120.2 68.2 %all-to-all-done.4 = f32[2,64,16,384]{3,2,0,1:T(8,128)S(1)} async-done(((f32[2,64,16,384]{3,2,0,1:T(8,128)}), f32[2,64,16,384]{3,2,0,1:T(8,128)S(1)}, u32[]{:S(2)}, u32[]{:S(2)}) %all-to-all-start.4) | async-done | bytes 3145760 | tf_op jit(solution)/shard_map/all_to_all | solution.py:137
  190.1 6.1 %all-to-all-start.3 = ((f32[2,64,16,384]{3,2,0,1:T(8,128)}), f32[2,64,16,384]{3,2,0,1:T(8,128)S(1)}, u32[]{:S(2)}, u32[]{:S(2)}) async-start(f32[2,64,16,384]{3,2,0,1:T(8,128)} %copy.41), calls=%async_computation.3 | async-start | bytes 6291456 | tf_op jit(solution)/shard_map/all_to_all | solution.py:136
  196.3 8.5 %fusion.16 = f32[2,16,384,64]{2,3,1,0:T(8,128)} fusion(f32[2,64,16,384]{3,2,0,1:T(8,128)} %copy-done.2), kind=kOutput, calls=%fused_computation.27 | convolution fusion | flops 604041216 | bytes 6291456 | tf_op jit(solution)/shard_map/qr,bkrsc->bkqsc/dot_general | solution.py:25
  204.8 6.6 %fusion.14 = f32[2,16,384,64]{2,3,1,0:T(8,128)} fusion(f32[2,64,16,384]{3,2,0,1:T(8,128)S(1)} %copy-done.3), kind=kOutput, calls=%fused_computation.25 | convolution fusion | flops 604037120 | bytes 6291456 | tf_op jit(solution)/shard_map/qr,bkrsc->bkqsc/dot_general | solution.py:25
  211.4 58.2 %all-to-all-done.3 = f32[2,64,16,384]{3,2,0,1:T(8,128)S(1)} async-done(((f32[2,64,16,384]{3,2,0,1:T(8,128)}), f32[2,64,16,384]{3,2,0,1:T(8,128)S(1)}, u32[]{:S(2)}, u32[]{:S(2)}) %all-to-all-start.3) | async-done | bytes 3145760 | tf_op jit(solution)/shard_map/all_to_all | solution.py:136
  269.7 7.5 %fusion.46 = f32[2,16,384,64]{2,3,1,0:T(8,128)S(1)} fusion(f32[2,16,384,64]{2,3,1,0:T(8,128)} %fusion.16, f32[2,64,16,384]{3,2,0,1:T(8,128)S(1)} %all-to-all-done.3), kind=kOutput, calls=%fused_computation.71 | convolution fusion | flops 604823552 | bytes 9437184 | tf_op jit(solution)/shard_map/qr,bkrsc->bkqsc/dot_general | solution.py:25
  277.2 6.2 %fusion.1 = (f32[2,64,16,384]{3,1,2,0:T(8,128)S(1)}, f32[2,64,16,384]{3,1,2,0:T(8,128)S(1)}) fusion(f32[2,16,384,64]{2,3,1,0:T(8,128)S(1)} %fusion.46, f32[64,16]{0,1:T(8,128)S(1)} %get-tuple-element.24, f32[64,16]{0,1:T(8,128)S(1)} %get-tuple-element.25, f32[2,16,384,64]{2,3,1,0:T(8,128)S(1)} %copy-done.4, f32[2,64,16,384]{3,2,0,1:T(8,128)S(1)} %all-to-all-done.3), kind=kOutput, calls=%fused_computation.4 | convolution fusion | flops 609546240 | bytes 15736832 | tf_op jit(solution)/shard_map/qr,bkrsc->bkqsc/dot_general | solution.py:25
  283.4 4.8 fusion.8
  288.3 4.7 fusion.6
  293.0 4.8 subtract_bitcast_fusion
  297.8 5.0 add_bitcast_fusion
  304.9 71.6 %all-reduce.4.cloned.1.call-done = (f32[2,1,64,16,128]{4,3,2,0,1:T(8,128)}, f32[2,1,64,16,128]{4,3,2,0,1:T(8,128)}) async-done(((f32[2,1,64,16,128]{4,3,2,0,1:T(8,128)}, f32[2,1,64,16,128]{4,3,2,0,1:T(8,128)}), (f32[2,1,64,16,128]{4,3,2,0,1:T(8,128)}, f32[2,1,64,16,128]{4,3,2,0,1:T(8,128)})) %all-reduce.4.cloned.1.call-update) | async-done | bytes 2097168 | tf_op jit(solution)/shard_map/psum | solution.py:149
  398.4 3.6 add_bitcast_fusion.2
  406.7 10.9 %all-to-all-start.6 = ((f32[2,1,1024,256]{3,0,1,2:T(2,128)}), f32[2,1,1024,256]{3,0,1,2:T(2,128)}, u32[]{:S(2)}, u32[]{:S(2)}) async-start(f32[2,1,1024,256]{3,0,1,2:T(2,128)} %copy.62), calls=%async_computation.6 | async-start | bytes 4194304 | tf_op jit(solution)/shard_map/all_to_all | solution.py:158
  420.5 48.2 %all-to-all-done.6 = f32[2,1,1024,256]{3,0,1,2:T(2,128)} async-done(((f32[2,1,1024,256]{3,0,1,2:T(2,128)}), f32[2,1,1024,256]{3,0,1,2:T(2,128)}, u32[]{:S(2)}, u32[]{:S(2)}) %all-to-all-start.6) | async-done | bytes 2097184 | tf_op jit(solution)/shard_map/all_to_all | solution.py:158
  468.7 6.2 %all-to-all-start.5 = ((f32[2,1,1024,256]{3,0,1,2:T(2,128)}), f32[2,1,1024,256]{3,0,1,2:T(2,128)}, u32[]{:S(2)}, u32[]{:S(2)}) async-start(f32[2,1,1024,256]{3,0,1,2:T(2,128)} %copy.59), calls=%async_computation.5 | async-start | bytes 4194304 | tf_op jit(solution)/shard_map/all_to_all | solution.py:157
  476.7 4.7 fusion.32
  484.7 41.2 %all-to-all-done.5 = f32[2,1,1024,256]{3,0,1,2:T(2,128)} async-done(((f32[2,1,1024,256]{3,0,1,2:T(2,128)}), f32[2,1,1024,256]{3,0,1,2:T(2,128)}, u32[]{:S(2)}, u32[]{:S(2)}) %all-to-all-start.5) | async-done | bytes 2097184 | tf_op jit(solution)/shard_map/all_to_all | solution.py:157
  531.4 3.6 add_bitcast_fusion.1
  536.4 5.8 all-to-all-start.7
  543.3 10.8 %all-to-all-done.7 = bf16[64,16,128]{2,1,0:T(8,128)(2,1)S(1)} async-done(((bf16[64,16,128]{2,1,0:T(8,128)(2,1)}), bf16[64,16,128]{2,1,0:T(8,128)(2,1)S(1)}, u32[]{:S(2)}, u32[]{:S(2)}) %all-to-all-start.7) | async-done | bytes 262176 | tf_op jit(solution)/shard_map/all_to_all | solution.py:165
  554.2 6.0 %all-to-all-start.8 = ((f32[64,16,128]{2,1,0:T(8,128)}), f32[64,16,128]{2,1,0:T(8,128)S(1)}, u32[]{:S(2)}, u32[]{:S(2)}) async-start(f32[64,16,128]{2,1,0:T(8,128)} %copy.68), calls=%async_computation.8 | async-start | bytes 1048576 | tf_op jit(solution)/shard_map/all_to_all | solution.py:167
  560.2 17.3 %all-to-all-done.8 = f32[64,16,128]{2,1,0:T(8,128)S(1)} async-done(((f32[64,16,128]{2,1,0:T(8,128)}), f32[64,16,128]{2,1,0:T(8,128)S(1)}, u32[]{:S(2)}, u32[]{:S(2)}) %all-to-all-start.8) | async-done | bytes 524320 | tf_op jit(solution)/shard_map/all_to_all | solution.py:167
  (61 shorter events, 56.9 us)
Async XLA Ops:
  7.2 10.0 %copy-start = (bf16[128,256]{1,0:T(8,128)(2,1)S(1)}, bf16[128,256]{1,0:T(8,128)(2,1)}, u32[]{:S(2)}) copy-start(bf16[128,256]{1,0:T(8,128)(2,1)} %param.7) | copy-start | bytes 196612
  7.2 35.7 %copy-start.8 = (bf16[1024,128]{1,0:T(8,128)(2,1)S(1)}, bf16[1024,128]{1,0:T(8,128)(2,1)}, u32[]{:S(2)}) copy-start(bf16[1024,128]{1,0:T(8,128)(2,1)} %param.6) | copy-start | bytes 786436
  60.7 18.4 %all-to-all-start.1 = ((bf16[64,16,128]{2,1,0:T(8,128)(2,1)}), bf16[64,16,128]{2,1,0:T(8,128)(2,1)S(1)}, u32[]{:S(2)}, u32[]{:S(2)}) async-start(bf16[64,16,128]{2,1,0:T(8,128)(2,1)} %bitcast.3), calls=%async_computation.1 | async-start | bytes 524288 | tf_op jit(solution)/shard_map/all_to_all | solution.py:121
  108.8 79.5 %all-to-all-start.4 = ((f32[2,64,16,384]{3,2,0,1:T(8,128)}), f32[2,64,16,384]{3,2,0,1:T(8,128)S(1)}, u32[]{:S(2)}, u32[]{:S(2)}) async-start(f32[2,64,16,384]{3,2,0,1:T(8,128)} %copy.43), calls=%async_computation.4 | async-start | bytes 6291456 | tf_op jit(solution)/shard_map/all_to_all | solution.py:137
  188.3 1.7 copy-start.2
  190.1 79.6 %all-to-all-start.3 = ((f32[2,64,16,384]{3,2,0,1:T(8,128)}), f32[2,64,16,384]{3,2,0,1:T(8,128)S(1)}, u32[]{:S(2)}, u32[]{:S(2)}) async-start(f32[2,64,16,384]{3,2,0,1:T(8,128)} %copy.41), calls=%async_computation.3 | async-start | bytes 6291456 | tf_op jit(solution)/shard_map/all_to_all | solution.py:136
  196.2 180.4 %all-reduce.4.cloned.1.call-start = ((), (), s32[]{:S(2)}) async-start(), calls=%async_computation.9 | async-start | bytes 4194304 | tf_op jit(solution)/shard_map/psum | solution.py:149
  196.3 8.5 %copy-start.3 = (f32[2,64,16,384]{3,2,0,1:T(8,128)S(1)}, f32[2,64,16,384]{3,2,0,1:T(8,128)}, u32[]{:S(2)}) copy-start(f32[2,64,16,384]{3,2,0,1:T(8,128)} %copy-done.2) | copy-start | bytes 9437188
  269.7 7.5 %copy-start.4 = (f32[2,16,384,64]{2,3,1,0:T(8,128)S(1)}, f32[2,16,384,64]{2,3,1,0:T(8,128)}, u32[]{:S(2)}) copy-start(f32[2,16,384,64]{2,3,1,0:T(8,128)} %fusion.14) | copy-start | bytes 9437188
  376.5 3.3 copy-start.7
  379.8 2.0 copy-start.6
  406.7 62.0 %all-to-all-start.6 = ((f32[2,1,1024,256]{3,0,1,2:T(2,128)}), f32[2,1,1024,256]{3,0,1,2:T(2,128)}, u32[]{:S(2)}, u32[]{:S(2)}) async-start(f32[2,1,1024,256]{3,0,1,2:T(2,128)} %copy.62), calls=%async_computation.6 | async-start | bytes 4194304 | tf_op jit(solution)/shard_map/all_to_all | solution.py:158
  468.7 57.2 %all-to-all-start.5 = ((f32[2,1,1024,256]{3,0,1,2:T(2,128)}), f32[2,1,1024,256]{3,0,1,2:T(2,128)}, u32[]{:S(2)}, u32[]{:S(2)}) async-start(f32[2,1,1024,256]{3,0,1,2:T(2,128)} %copy.59), calls=%async_computation.5 | async-start | bytes 4194304 | tf_op jit(solution)/shard_map/all_to_all | solution.py:157
  525.9 2.2 copy-start.5
  536.4 17.8 %all-to-all-start.7 = ((bf16[64,16,128]{2,1,0:T(8,128)(2,1)}), bf16[64,16,128]{2,1,0:T(8,128)(2,1)S(1)}, u32[]{:S(2)}, u32[]{:S(2)}) async-start(bf16[64,16,128]{2,1,0:T(8,128)(2,1)} %copy.67), calls=%async_computation.7 | async-start | bytes 524288 | tf_op jit(solution)/shard_map/all_to_all | solution.py:165
  542.2 36.9 %copy-start.1 = (bf16[128,256]{1,0:T(8,128)(2,1)S(1)}, bf16[128,256]{1,0:T(8,128)(2,1)}, u32[]{:S(2)}) copy-start(bf16[128,256]{1,0:T(8,128)(2,1)} %param.7) | copy-start | bytes 196612
  554.2 23.4 %all-to-all-start.8 = ((f32[64,16,128]{2,1,0:T(8,128)}), f32[64,16,128]{2,1,0:T(8,128)S(1)}, u32[]{:S(2)}, u32[]{:S(2)}) async-start(f32[64,16,128]{2,1,0:T(8,128)} %copy.68), calls=%async_computation.8 | async-start | bytes 1048576 | tf_op jit(solution)/shard_map/all_to_all | solution.py:167
Sparse Core Ops, SparseCore 0:
  304.7 71.7 all-reduce.3
where the time goes:
time: 590 us; the launch traced here: 586 us
  waiting for transfers between devices  327 us (55%)
  matrix products  113 us (19%)
  blocking collectives  53.2 us (9%)
  starting transfers between devices  47.6 us (8%)
  local copies, waits for them, and re-layouts  26.9 us (5%)
  between operations  14.7 us (2%)
    dot_general x24, matrix products, product(): return jnp.einsum(pattern, first_op, second_op, precision=precise_mode)  113 us
    psum x1, waiting for transfers between devices, per_device(): dk_real, dk_imag = lax.psum((dk_real, dk_imag), 'rep')  71.6 us
    all_to_all x1, waiting for transfers between devices, per_device(): lax.all_to_all(imag_part, 'seq', split_axis=1, concat_axis=2, tiled=True)  68.2 us
    all_to_all x1, waiting for transfers between devices, per_device(): lax.all_to_all(real_part, 'seq', split_axis=1, concat_axis=2, tiled=True)  58.2 us
    all_to_all x1, waiting for transfers between devices, per_device(): lax.all_to_all(imag_part, 'seq', split_axis=2, concat_axis=1, tiled=True)  48.2 us
    all_to_all x1, waiting for transfers between devices, per_device(): lax.all_to_all(real_part, 'seq', split_axis=2, concat_axis=1, tiled=True)  41.2 us
    all_to_all x1, blocking collectives, per_device(): lax.all_to_all(signals[0], 'seq', split_axis=0, concat_axis=0, tiled=True)  25.4 us
    all_to_all x1, blocking collectives, per_device(): lax.all_to_all(signals[2], 'seq', split_axis=0, concat_axis=0, tiled=True)  17.8 us
  transfers between devices with their start and end apart: 8, of which 8 were waited for; matrix products, arithmetic and copies ran while one was open for 6% of the time, Pallas kernels for 0%

commit v1 on v0

--- a/solution.py
+++ b/solution.py
@@ -134,7 +134,12 @@
     )
     real_part, imag_part = (
         lax.all_to_all(real_part, "seq", split_axis=1, concat_axis=2, tiled=True),
-        lax.all_to_all(imag_part, "seq", split_axis=1, concat_axis=2, tiled=True),
+        jnp.concatenate(
+            lax.all_to_all(
+                jnp.stack(jnp.split(imag_part, lax.axis_size("seq"), axis=1)), "seq", 0, 0
+            ),
+            axis=2,
+        ),
     )
     real_part, imag_part = rows_forward(real_part, imag_part)
     part_width = real_part.shape[-1] // 3

time: 590 us -> 617 us (1.046)
  local copies, waits for them, and re-layouts: 26.9 us -> 63.8 us
  matrix products: 113 us -> 101 us
    unnamed x20 -> x77, local copies, waits for them, and re-layouts: 3.56 us -> 43.4 us
    dot_general x24, matrix products: 113 us -> 100 us  [product(): return jnp.einsum(pattern, first_op, second_op, precision=precise_mode)]
  transfers between devices with their start and end apart: 8 -> 8, of which waited for: 8 -> 8; matrix products, arithmetic and copies ran while one was open for 6% -> 5% of each run, Pallas kernels for 0% -> 0%
where the time goes in v1:
time: 617 us; the launch traced here: 613 us
  waiting for transfers between devices  329 us (53%)
  matrix products  101 us (16%)
  local copies, waits for them, and re-layouts  63.8 us (10%)
  blocking collectives  53.4 us (9%)
  starting transfers between devices  48.3 us (8%)
  between operations  14.7 us (2%)
    dot_general x24, matrix products, product(): return jnp.einsum(pattern, first_op, second_op, precision=precise_mode)  100 us
    psum x1, waiting for transfers between devices, per_device(): dk_real, dk_imag = lax.psum((dk_real, dk_imag), 'rep')  71.6 us
    all_to_all x1, waiting for transfers between devices, per_device(): lax.all_to_all(jnp.stack(jnp.split(imag_part, lax.axis_size('seq'), axis=...  68.1 us
    all_to_all x1, waiting for transfers between devices, per_device(): lax.all_to_all(real_part, 'seq', split_axis=1, concat_axis=2, tiled=True)  59.8 us
    all_to_all x1, waiting for transfers between devices, per_device(): lax.all_to_all(imag_part, 'seq', split_axis=2, concat_axis=1, tiled=True)  48.2 us
    unnamed x77, local copies, waits for them, and re-layouts  43.4 us
    all_to_all x1, waiting for transfers between devices, per_device(): lax.all_to_all(real_part, 'seq', split_axis=2, concat_axis=1, tiled=True)  41.2 us
    all_to_all x1, blocking collectives, per_device(): lax.all_to_all(signals[0], 'seq', split_axis=0, concat_axis=0, tiled=True)  25.4 us
  transfers between devices with their start and end apart: 8, of which 8 were waited for; matrix products, arithmetic and copies ran while one was open for 5% of the time, Pallas kernels for 0%

profile of v1, /device:TPU:1, one launch (start us, length us, event | category | flops | bytes accessed | tf_op | source)
XLA Modules:
  0.0 612.7 jit_solution(4259107944136770866)
XLA Ops:
  7.2 9.9 %all-gather = bf16[1,1024,256]{2,1,0:T(8,128)(2,1)S(1)} all-gather(bf16[1,1024,128]{2,1,0:T(8,128)(2,1)} %param.5), channel_id=2, replica_groups=mesh['rep'=2,'seq'=64,'chan'=2] {'chan'}, dimensions={2}, use_global_device_ids=true | all-gather | bytes 786432 | tf_op jit(solution)/shard_map/all_gather | solution.py:110
  17.4 25.4 %all_to_all.80 = bf16[64,16,128]{2,1,0:T(8,128)(2,1)S(1)} all-to-all(bf16[64,16,128]{2,1,0:T(8,128)(2,1)S(1)} %bitcast.508), channel_id=1, replica_groups=mesh['rep'=2,'seq'=64,'chan'=2] {'seq'}, dimensions={0} | all-to-all | bytes 524288 | tf_op jit(solution)/shard_map/all_to_all | solution.py:120
  42.9 18.0 %all_to_all.81 = bf16[64,16,128]{2,1,0:T(8,128)(2,1)S(1)} all-to-all(bf16[64,16,128]{2,1,0:T(8,128)(2,1)} %bitcast.509), channel_id=1, replica_groups=mesh['rep'=2,'seq'=64,'chan'=2] {'seq'}, dimensions={0} | all-to-all | bytes 524288 | tf_op jit(solution)/shard_map/all_to_all | solution.py:122
  60.9 6.7 %all-to-all-start.1 = ((bf16[64,16,128]{2,1,0:T(8,128)(2,1)}), bf16[64,16,128]{2,1,0:T(8,128)(2,1)S(1)}, u32[]{:S(2)}, u32[]{:S(2)}) async-start(bf16[64,16,128]{2,1,0:T(8,128)(2,1)} %bitcast.510), calls=%async_computation.1 | async-start | bytes 524288 | tf_op jit(solution)/shard_map/all_to_all | solution.py:121
  67.9 11.5 %all-to-all-done.1 = bf16[64,16,128]{2,1,0:T(8,128)(2,1)S(1)} async-done(((bf16[64,16,128]{2,1,0:T(8,128)(2,1)}), bf16[64,16,128]{2,1,0:T(8,128)(2,1)S(1)}, u32[]{:S(2)}, u32[]{:S(2)}) %all-to-all-start.1) | async-done | bytes 262176 | tf_op jit(solution)/shard_map/all_to_all | solution.py:121
  88.0 5.7 fusion.8
  136.0 6.0 all-to-all-start.4
  142.0 5.4 copy.45
  147.4 68.1 %all-to-all-done.4 = f32[64,2,1,16,384]{4,2,3,1,0:T(1,128)S(1)} async-done(((f32[64,2,1,16,384]{4,2,3,1,0:T(1,128)}), f32[64,2,1,16,384]{4,2,3,1,0:T(1,128)S(1)}, u32[]{:S(2)}, u32[]{:S(2)}) %all-to-all-start.4) | async-done | bytes 3145760 | tf_op jit(solution)/shard_map/all_to_all | solution.py:138
  215.5 6.2 %all-to-all-start.3 = ((f32[2,64,16,384]{3,2,0,1:T(8,128)}), f32[2,64,16,384]{3,2,0,1:T(8,128)}, u32[]{:S(2)}, u32[]{:S(2)}) async-start(f32[2,64,16,384]{3,2,0,1:T(8,128)} %copy.45), calls=%async_computation.3 | async-start | bytes 6291456 | tf_op jit(solution)/shard_map/all_to_all | solution.py:136
  222.3 6.6 %fusion.2 = f32[2,16,384,64]{2,3,1,0:T(8,128)} fusion(f32[2,1,64,16,384]{4,1,3,0,2:T(1,128)S(1)} %bitcast.488), kind=kOutput, calls=%fused_computation.3 | convolution fusion | flops 604041216 | bytes 6291456 | tf_op jit(solution)/shard_map/qr,bkrsc->bkqsc/dot_general | solution.py:25
  228.9 6.6 %fusion = f32[2,16,384,64]{2,3,1,0:T(8,128)} fusion(f32[2,1,64,16,384]{4,1,3,0,2:T(1,128)S(1)} %bitcast.489), kind=kOutput, calls=%fused_computation.1 | convolution fusion | flops 604037120 | bytes 6291456 | tf_op jit(solution)/shard_map/qr,bkrsc->bkqsc/dot_general | solution.py:25
  235.4 59.8 %all-to-all-done.3 = f32[2,64,16,384]{3,2,0,1:T(8,128)} async-done(((f32[2,64,16,384]{3,2,0,1:T(8,128)}), f32[2,64,16,384]{3,2,0,1:T(8,128)}, u32[]{:S(2)}, u32[]{:S(2)}) %all-to-all-start.3) | async-done | bytes 3145760 | tf_op jit(solution)/shard_map/all_to_all | solution.py:136
  295.2 8.0 %fusion.48 = f32[2,16,384,64]{2,3,1,0:T(8,128)S(1)} fusion(f32[2,16,384,64]{2,3,1,0:T(8,128)} %fusion.2, f32[2,64,16,384]{3,2,0,1:T(8,128)} %all-to-all-done.3), kind=kOutput, calls=%fused_computation.73 | convolution fusion | flops 604823552 | bytes 9437184 | tf_op jit(solution)/shard_map/qr,bkrsc->bkqsc/dot_general | solution.py:25
  303.2 6.9 %fusion.5 = (f32[2,64,16,384]{3,1,2,0:T(8,128)S(1)}, f32[2,64,16,384]{3,1,2,0:T(8,128)S(1)}) fusion(f32[2,16,384,64]{2,3,1,0:T(8,128)S(1)} %fusion.48, f32[64,16]{0,1:T(8,128)S(1)} %get-tuple-element.24, f32[64,16]{0,1:T(8,128)S(1)} %get-tuple-element.25, f32[2,16,384,64]{2,3,1,0:T(8,128)S(1)} %copy-done.2, f32[2,64,16,384]{3,2,0,1:T(8,128)} %all-to-all-done.3), kind=kOutput, calls=%fused_computation.8 | convolution fusion | flops 609546240 | bytes 15736832 | tf_op jit(solution)/shard_map/qr,bkrsc->bkqsc/dot_general | solution.py:25
  310.1 4.7 fusion.14
  314.7 4.7 fusion.12
  319.4 5.2 subtract_bitcast_fusion
  324.7 4.8 add_bitcast_fusion
  331.5 71.6 %all-reduce.4.cloned.1.call-done = (f32[2,1,64,16,128]{4,3,2,0,1:T(8,128)}, f32[2,1,64,16,128]{4,3,2,0,1:T(8,128)}) async-done(((f32[2,1,64,16,128]{4,3,2,0,1:T(8,128)}, f32[2,1,64,16,128]{4,3,2,0,1:T(8,128)}), (f32[2,1,64,16,128]{4,3,2,0,1:T(8,128)}, f32[2,1,64,16,128]{4,3,2,0,1:T(8,128)})) %all-reduce.4.cloned.1.call-update) | async-done | bytes 2097168 | tf_op jit(solution)/shard_map/psum | solution.py:154
  420.1 3.7 subtract_bitcast_fusion.2
  425.1 3.5 add_bitcast_fusion.2
  433.3 10.8 %all-to-all-start.6 = ((f32[2,1,1024,256]{3,0,1,2:T(2,128)}), f32[2,1,1024,256]{3,0,1,2:T(2,128)}, u32[]{:S(2)}, u32[]{:S(2)}) async-start(f32[2,1,1024,256]{3,0,1,2:T(2,128)} %copy.65), calls=%async_computation.6 | async-start | bytes 4194304 | tf_op jit(solution)/shard_map/all_to_all | solution.py:163
  447.1 48.2 %all-to-all-done.6 = f32[2,1,1024,256]{3,0,1,2:T(2,128)} async-done(((f32[2,1,1024,256]{3,0,1,2:T(2,128)}), f32[2,1,1024,256]{3,0,1,2:T(2,128)}, u32[]{:S(2)}, u32[]{:S(2)}) %all-to-all-start.6) | async-done | bytes 2097184 | tf_op jit(solution)/shard_map/all_to_all | solution.py:163
  495.3 6.2 %all-to-all-start.5 = ((f32[2,1,1024,256]{3,0,1,2:T(2,128)}), f32[2,1,1024,256]{3,0,1,2:T(2,128)}, u32[]{:S(2)}, u32[]{:S(2)}) async-start(f32[2,1,1024,256]{3,0,1,2:T(2,128)} %copy.62), calls=%async_computation.5 | async-start | bytes 4194304 | tf_op jit(solution)/shard_map/all_to_all | solution.py:162
  503.2 4.7 fusion.34
  511.2 41.2 %all-to-all-done.5 = f32[2,1,1024,256]{3,0,1,2:T(2,128)} async-done(((f32[2,1,1024,256]{3,0,1,2:T(2,128)}), f32[2,1,1024,256]{3,0,1,2:T(2,128)}, u32[]{:S(2)}, u32[]{:S(2)}) %all-to-all-start.5) | async-done | bytes 2097184 | tf_op jit(solution)/shard_map/all_to_all | solution.py:162
  558.0 3.6 add_bitcast_fusion.1
  562.9 5.8 all-to-all-start.7
  569.9 10.9 %all-to-all-done.7 = bf16[64,16,128]{2,1,0:T(8,128)(2,1)S(1)} async-done(((bf16[64,16,128]{2,1,0:T(8,128)(2,1)}), bf16[64,16,128]{2,1,0:T(8,128)(2,1)S(1)}, u32[]{:S(2)}, u32[]{:S(2)}) %all-to-all-start.7) | async-done | bytes 262176 | tf_op jit(solution)/shard_map/all_to_all | solution.py:170
  580.7 6.0 all-to-all-start.8
  586.8 17.3 %all-to-all-done.8 = f32[64,16,128]{2,1,0:T(8,128)S(1)} async-done(((f32[64,16,128]{2,1,0:T(8,128)}), f32[64,16,128]{2,1,0:T(8,128)S(1)}, u32[]{:S(2)}, u32[]{:S(2)}) %all-to-all-start.8) | async-done | bytes 524320 | tf_op jit(solution)/shard_map/all_to_all | solution.py:172
  (118 shorter events, 94.1 us)
Async XLA Ops:
  7.2 10.0 %copy-start = (bf16[128,256]{1,0:T(8,128)(2,1)S(1)}, bf16[128,256]{1,0:T(8,128)(2,1)}, u32[]{:S(2)}) copy-start(bf16[128,256]{1,0:T(8,128)(2,1)} %param.7) | copy-start | bytes 196612
  60.9 18.5 %all-to-all-start.1 = ((bf16[64,16,128]{2,1,0:T(8,128)(2,1)}), bf16[64,16,128]{2,1,0:T(8,128)(2,1)S(1)}, u32[]{:S(2)}, u32[]{:S(2)}) async-start(bf16[64,16,128]{2,1,0:T(8,128)(2,1)} %bitcast.510), calls=%async_computation.1 | async-start | bytes 524288 | tf_op jit(solution)/shard_map/all_to_all | solution.py:121
  136.0 79.5 %all-to-all-start.4 = ((f32[64,2,1,16,384]{4,2,3,1,0:T(1,128)}), f32[64,2,1,16,384]{4,2,3,1,0:T(1,128)S(1)}, u32[]{:S(2)}, u32[]{:S(2)}) async-start(f32[64,2,1,16,384]{4,2,3,1,0:T(1,128)} %constant_dynamic-update-slice_fusion), calls=%async_computation.4 | async-start | bytes 6291456 | tf_op jit(solution)/shard_map/all_to_all | solution.py:138
  215.5 79.7 %all-to-all-start.3 = ((f32[2,64,16,384]{3,2,0,1:T(8,128)}), f32[2,64,16,384]{3,2,0,1:T(8,128)}, u32[]{:S(2)}, u32[]{:S(2)}) async-start(f32[2,64,16,384]{3,2,0,1:T(8,128)} %copy.45), calls=%async_computation.3 | async-start | bytes 6291456 | tf_op jit(solution)/shard_map/all_to_all | solution.py:136
  221.8 181.4 %all-reduce.4.cloned.1.call-start = ((), (), s32[]{:S(2)}) async-start(), calls=%async_computation.9 | async-start | bytes 4194304 | tf_op jit(solution)/shard_map/psum | solution.py:154
  235.4 67.7 %copy-start.2 = (f32[2,16,384,64]{2,3,1,0:T(8,128)S(1)}, f32[2,16,384,64]{2,3,1,0:T(8,128)}, u32[]{:S(2)}) copy-start(f32[2,16,384,64]{2,3,1,0:T(8,128)} %fusion) | copy-start | bytes 9437188
  403.2 3.3 copy-start.5
  406.5 2.0 copy-start.4
  433.3 62.0 %all-to-all-start.6 = ((f32[2,1,1024,256]{3,0,1,2:T(2,128)}), f32[2,1,1024,256]{3,0,1,2:T(2,128)}, u32[]{:S(2)}, u32[]{:S(2)}) async-start(f32[2,1,1024,256]{3,0,1,2:T(2,128)} %copy.65), calls=%async_computation.6 | async-start | bytes 4194304 | tf_op jit(solution)/shard_map/all_to_all | solution.py:163
  495.3 57.2 %all-to-all-start.5 = ((f32[2,1,1024,256]{3,0,1,2:T(2,128)}), f32[2,1,1024,256]{3,0,1,2:T(2,128)}, u32[]{:S(2)}, u32[]{:S(2)}) async-start(f32[2,1,1024,256]{3,0,1,2:T(2,128)} %copy.62), calls=%async_computation.5 | async-start | bytes 4194304 | tf_op jit(solution)/shard_map/all_to_all | solution.py:162
  552.5 2.2 copy-start.3
  561.6 44.0 %copy-start.1 = (bf16[128,256]{1,0:T(8,128)(2,1)S(1)}, bf16[128,256]{1,0:T(8,128)(2,1)}, u32[]{:S(2)}) copy-start(bf16[128,256]{1,0:T(8,128)(2,1)} %param.7) | copy-start | bytes 196612
  562.9 17.8 %all-to-all-start.7 = ((bf16[64,16,128]{2,1,0:T(8,128)(2,1)}), bf16[64,16,128]{2,1,0:T(8,128)(2,1)S(1)}, u32[]{:S(2)}, u32[]{:S(2)}) async-start(bf16[64,16,128]{2,1,0:T(8,128)(2,1)} %copy.70), calls=%async_computation.7 | async-start | bytes 524288 | tf_op jit(solution)/shard_map/all_to_all | solution.py:170
  580.7 23.4 %all-to-all-start.8 = ((f32[64,16,128]{2,1,0:T(8,128)}), f32[64,16,128]{2,1,0:T(8,128)S(1)}, u32[]{:S(2)}, u32[]{:S(2)}) async-start(f32[64,16,128]{2,1,0:T(8,128)} %copy.71), calls=%async_computation.8 | async-start | bytes 1048576 | tf_op jit(solution)/shard_map/all_to_all | solution.py:172
Sparse Core Ops, SparseCore 0:
  331.4 71.7 all-reduce.3
